TPU v7x, 128 devices: a whole 4x4x4 slice. The times are simulated.
128 devices in a mesh: grp: 4 (over z), dev: 32 (over x, y, core).
Axes of the slice: x: 4, y: 4, z: 4, core: 2. Of those that a mesh axis runs over, the one named last changes fastest.
Arguments:
- fitted_factors: bfloat16 [9000, 32768], P(None, 'dev'), may hold values from -0.0625 to 0.0625
- panel_blocks: int32 [16], P('grp'), may hold values from 0 to 127
- kept_tiles: int32 [16, 256], P('grp', 'dev'), may hold values 0 or 1
- tile_owner: int32 [4, 32, 32, 1], P('grp', 'dev'), may hold values from 0 to 31; in each aligned block of 32 rows (0 to 31, 32 to 63, ..., all dimensions but the last counted through in order) at most 2 rows name the same one
Outputs:
- exported: bfloat16 [4, 32, 64, 256, 128], P('grp', 'dev')
Inputs may be any that keep to these rules, and one draw needn't show every extreme that they name: `tile_owner`: in each device's list of 32 tiles no owner appears more than 2 times, and some owner appears exactly 2 times.
All inputs are finite; a program needn't handle non-finite values. No bound on the sum of `kept_tiles` on one device may be relied on, other than what follows from the above.
Results may differ from a plain program's by a relative error of at most 0.0015.
Values may be sent and summed in bfloat16 or wider, within the bound.
No kernel may reach another device: no remote copies, remote signals or barrier semaphores. Data moves between devices by JAX's collectives and lax.ppermute only.
A program may use at most 128 MiB of HBM per device.

v0:
```python
import jax
import jax.numpy as jnp
from jax import lax
from jax.sharding import PartitionSpec as P

PB = 256
CB = 128


def broadcast(value, axis, source):
    kept = jnp.where(lax.axis_index(axis) == source, value, 0).astype(value.dtype)
    return lax.psum(kept, axis)


def slot_ranks(owners):
    count = owners.shape[-1]
    same_owner = owners[..., :, None] == owners[..., None, :]
    earlier = jnp.arange(count)[None, :] < jnp.arange(count)[:, None]
    return jnp.sum((same_owner & earlier).astype(jnp.int32), axis=-1)


def body(fitted_factors, panel_blocks, kept_tiles, tile_owner):
    local_cols = fitted_factors.shape[1]
    blocks_here = local_cols // CB
    panel_count = panel_blocks.shape[0]
    dev_count = lax.axis_size("dev")
    tile_list = []
    for panel_idx in range(panel_count):
        first_col = panel_blocks[panel_idx] * PB
        root_dev = first_col // local_cols
        start_col = first_col % local_cols
        own_piece = lax.dynamic_slice_in_dim(fitted_factors, start_col, PB, 1)
        panel_cols = broadcast(own_piece, "dev", root_dev)
        kept_row = kept_tiles[panel_idx]
        product = lax.dot_general(
            panel_cols, fitted_factors, (((0,), (0,)), ((), ())), preferred_element_type=jnp.float32
        )
        product = product.reshape(PB, blocks_here, CB) * kept_row.astype(jnp.float32)[None, :, None]
        panel_tiles = jnp.transpose(product.astype(jnp.bfloat16), (1, 0, 2))
        tile_list.append(panel_tiles)
    tile_set = jnp.concatenate(tile_list, axis=0)
    tile_count = tile_set.shape[0]
    owners = tile_owner[0, 0, :, 0]
    ranks = slot_ranks(owners)
    capacity = max(2, 2 * tile_count // dev_count)
    send_buffer = jnp.zeros((dev_count * capacity, PB, CB), jnp.bfloat16)
    send_buffer = send_buffer.at[owners * capacity + ranks].set(tile_set)
    received = lax.all_to_all(
        send_buffer.reshape(dev_count, capacity, PB, CB),
        "dev",
        split_axis=0,
        concat_axis=0,
        tiled=True,
    )
    return received.reshape(1, 1, dev_count * capacity, PB, CB)


def solution(mesh):
    placed = (P(None, "dev"), P("grp"), P("grp", "dev"), P("grp", "dev", None, None))
    return jax.shard_map(
        body,
        mesh=mesh,
        in_specs=placed,
        out_specs=P("grp", "dev", None, None, None),
        check_vma=False,
    )
```

profile of v0, /device:TPU:1, one launch (start us, length us, event | category | flops | bytes accessed | tf_op | source)
XLA Modules:
  0.0 329.7 jit_solution(11810633867015240483)
XLA Ops:
  6.5 0.0 all-reduce.3.cloned.1.call-start
  6.5 1.4 fusion.10
  10.6 21.7 %dynamic-slice_select_fusion.3 = (bf16[9000,256]{1,0:T(8,128)(2,1)}, bf16[9000,256]{1,0:T(8,128)(2,1)}, bf16[9000,256]{1,0:T(8,128)(2,1)}, bf16[9000,256]{1,0:T(8,128)(2,1)}) fusion(bf16[9000,1024]{1,0:T(8,128)(2,1)} %param.4, s32[]{:T(128)S(6)} %select_n.84, pred[]{:T(512)S(6)} %eq.36, s32[]{:T(128)S(6)} %select_n.94, pred[]{:T(512)S(6)} %eq.38, ...), kind=kLoop, calls=%fused_computation.4 | loop fusion | flops 9216000 | bytes 36864020 | tf_op jit(solution)/shard_map/jit(_where)/select_n | solution.py:11
  32.4 0.0 copy-start.3
  32.4 0.0 copy-start.2
  32.4 0.0 all-reduce.3.cloned.1.call-update
  32.4 0.6 copy-done.3
  33.0 0.2 convert_reduce_fusion
  33.2 0.0 copy-done.2
  33.2 185.9 %all-reduce.3.cloned.1.call-done = (bf16[9000,256]{1,0:T(8,128)(2,1)}, bf16[9000,256]{1,0:T(8,128)(2,1)}, bf16[9000,256]{1,0:T(8,128)(2,1)}, bf16[9000,256]{1,0:T(8,128)(2,1)}) async-done(((bf16[9000,256]{1,0:T(8,128)(2,1)}, bf16[9000,256]{1,0:T(8,128)(2,1)}, bf16[9000,256]{1,0:T(8,128)(2,1)}, bf16[9000,256]{1,0:T(8,128)(2,1)}), (bf16[9000,256]{1,0:T(8,128)(2,1)}, bf16[9000,256]{1,0:T(8,128)(2,1)}, ...) | async-done | bytes 18432016 | tf_op jit(solution)/shard_map/psum | solution.py:12
  219.1 0.0 slice-start
  219.1 0.0 slice-start.1
  219.1 0.0 slice-start.2
  219.1 0.0 slice-start.7
  219.1 11.2 %convolution_bitcast_fusion.2 = f32[32,8,8,128]{3,2,1,0:T(8,128)} fusion(bf16[9000,256]{1,0:T(8,128)(2,1)} %get-tuple-element.7, bf16[9000,1024]{1,0:T(8,128)(2,1)} %param.4), kind=kOutput, calls=%fused_computation.8 | convolution fusion | flops 4718592000 | bytes 24088576 | tf_op jit(solution)/shard_map/dot_general | solution.py:35
  230.3 0.0 slice-start.3
  230.3 0.0 slice-start.4
  230.3 0.0 slice-start.8
  230.3 0.0 slice-start.5
  230.3 11.6 %convolution_bitcast_fusion.3 = f32[32,8,8,128]{3,2,1,0:T(8,128)} fusion(bf16[9000,256]{1,0:T(8,128)(2,1)} %get-tuple-element.8, bf16[9000,1024]{1,0:T(8,128)(2,1)} %param.4), kind=kOutput, calls=%fused_computation.9 | convolution fusion | flops 4718592000 | bytes 24088576 | tf_op jit(solution)/shard_map/dot_general | solution.py:35
  241.9 0.0 slice-done
  241.9 0.0 slice-done.1
  241.9 0.0 slice-done.2
  241.9 0.0 slice-done.7
  241.9 0.0 slice-done.3
  241.9 0.0 slice-done.4
  241.9 0.0 slice-done.8
  242.0 0.0 slice-start.6
  242.0 6.0 %convolution_bitcast_fusion = f32[32,8,8,128]{3,2,1,0:T(8,128)S(1)} fusion(bf16[9000,256]{1,0:T(8,128)(2,1)S(1)} %bitcast.78, bf16[9000,1024]{1,0:T(8,128)(2,1)S(1)} %bitcast.72), kind=kOutput, calls=%fused_computation.6 | convolution fusion | flops 4718592000 | bytes 24088576 | tf_op jit(solution)/shard_map/dot_general | solution.py:35
  248.0 0.0 slice-done.5
  248.0 0.0 slice-done.6
  248.0 0.0 copy-start
  248.0 0.0 copy-start.1
  248.0 5.9 %convolution_bitcast_fusion.1 = f32[32,8,8,128]{3,2,1,0:T(8,128)S(1)} fusion(bf16[9000,256]{1,0:T(8,128)(2,1)S(1)} %bitcast.76, bf16[9000,1024]{1,0:T(8,128)(2,1)S(1)} %bitcast.72), kind=kOutput, calls=%fused_computation.7 | convolution fusion | flops 4718592000 | bytes 24088576 | tf_op jit(solution)/shard_map/dot_general | solution.py:35
  254.0 0.0 copy-done
  254.0 0.0 copy-done.1
  254.0 0.3 fusion.4
  254.3 0.3 fusion.6
  254.6 0.3 pad_maximum_fusion
  254.9 3.0 broadcast_in_dim.9
  257.9 5.3 %scatter_fusion = bf16[64,256,128]{2,1,0:T(8,128)(2,1)} fusion(bf16[64,256,128]{2,1,0:T(8,128)(2,1)} %broadcast_in_dim.9, s32[32]{0:T(128)S(1)} %fusion.9, bf16[32,256,128]{2,1,0:T(8,128)(2,1)S(1)} %pad_maximum_fusion), kind=kCustom, calls=%fused_computation | custom fusion | bytes 6291584 | tf_op jit(solution)/shard_map/scatter | solution.py:47
  263.2 57.6 %all_to_all.5 = bf16[32,2,256,128]{3,2,1,0:T(8,128)(2,1)S(1)} all-to-all(bf16[32,2,256,128]{3,2,1,0:T(8,128)(2,1)} %bitcast.73), channel_id=1, replica_groups=mesh['grp'=4,'dev'=32] {'dev'}, dimensions={0} | all-to-all | bytes 8388608 | tf_op jit(solution)/shard_map/all_to_all | solution.py:48
  320.8 2.0 copy.35
  (5 shorter events, 0.0 us)
Async XLA Ops:
  6.5 212.6 %all-reduce.3.cloned.1.call-start = ((), (), s32[]{:S(2)}) async-start(), calls=%async_computation.1 | async-start | bytes 36864000 | tf_op jit(solution)/shard_map/psum | solution.py:12
  32.4 0.7 copy-start.3
  32.4 0.8 copy-start.2
  219.1 22.8 %slice-start = ((s8[18432000]{0:T(1024)(128)(4,1)}), s8[4194304]{0:T(1024)(128)(4,1)S(1)}, s32[]{:S(2)}) async-start(s8[18432000]{0:T(1024)(128)(4,1)} %bitcast.71), calls=%async_computation.2 | async-start | bytes 8388608
  219.1 22.8 %slice-start.1 = ((s8[18432000]{0:T(1024)(128)(4,1)}), s8[4194304]{0:T(1024)(128)(4,1)S(1)}, s32[]{:S(2)}) async-start(s8[18432000]{0:T(1024)(128)(4,1)} %bitcast.71), calls=%async_computation.3 | async-start | bytes 8388608
  219.1 22.8 %slice-start.2 = ((s8[18432000]{0:T(1024)(128)(4,1)}), s8[4194304]{0:T(1024)(128)(4,1)S(1)}, s32[]{:S(2)}) async-start(s8[18432000]{0:T(1024)(128)(4,1)} %bitcast.71), calls=%async_computation.4 | async-start | bytes 8388608
  219.1 22.8 %slice-start.7 = ((s8[4608000]{0:T(1024)(128)(4,1)}), s8[4194304]{0:T(1024)(128)(4,1)S(1)}, s32[]{:S(2)}) async-start(s8[4608000]{0:T(1024)(128)(4,1)} %bitcast.77), calls=%async_computation.9 | async-start | bytes 8388608
  230.3 11.7 %slice-start.3 = ((s8[18432000]{0:T(1024)(128)(4,1)}), s8[4194304]{0:T(1024)(128)(4,1)S(1)}, s32[]{:S(2)}) async-start(s8[18432000]{0:T(1024)(128)(4,1)} %bitcast.71), calls=%async_computation.5 | async-start | bytes 8388608
  230.3 11.7 %slice-start.4 = ((s8[18432000]{0:T(1024)(128)(4,1)}), s8[1654784]{0:T(1024)(128)(4,1)S(1)}, s32[]{:S(2)}) async-start(s8[18432000]{0:T(1024)(128)(4,1)} %bitcast.71), calls=%async_computation.6 | async-start | bytes 3309568
  230.3 11.7 %slice-start.8 = ((s8[4608000]{0:T(1024)(128)(4,1)}), s8[413696]{0:T(1024)(128)(4,1)S(1)}, s32[]{:S(2)}) async-start(s8[4608000]{0:T(1024)(128)(4,1)} %bitcast.77), calls=%async_computation.10 | async-start | bytes 827392
  230.3 17.7 %slice-start.5 = ((s8[4608000]{0:T(1024)(128)(4,1)}), s8[4194304]{0:T(1024)(128)(4,1)S(1)}, s32[]{:S(2)}) async-start(s8[4608000]{0:T(1024)(128)(4,1)} %bitcast.75), calls=%async_computation.7 | async-start | bytes 8388608
  242.0 6.1 %slice-start.6 = ((s8[4608000]{0:T(1024)(128)(4,1)}), s8[413696]{0:T(1024)(128)(4,1)S(1)}, s32[]{:S(2)}) async-start(s8[4608000]{0:T(1024)(128)(4,1)} %bitcast.75), calls=%async_computation.8 | async-start | bytes 827392
  248.0 6.0 %copy-start = (f32[32,8,8,128]{3,2,1,0:T(8,128)S(1)}, f32[32,8,8,128]{3,2,1,0:T(8,128)}, u32[]{:S(2)}) copy-start(f32[32,8,8,128]{3,2,1,0:T(8,128)} %convolution_bitcast_fusion.2) | copy-start | bytes 3145732
  248.0 6.0 %copy-start.1 = (f32[32,8,8,128]{3,2,1,0:T(8,128)S(1)}, f32[32,8,8,128]{3,2,1,0:T(8,128)}, u32[]{:S(2)}) copy-start(f32[32,8,8,128]{3,2,1,0:T(8,128)} %convolution_bitcast_fusion.3) | copy-start | bytes 3145732
Sparse Core Ops, SparseCore 0:
  32.5 186.5 all-reduce.2
where the time goes:
time: 330 us
  waiting for transfers between devices  186 us (56%)
  blocking collectives  57.6 us (17%)
  matrix products  34.7 us (11%)
  other arithmetic  22.8 us (7%)
  between operations  16.2 us (5%)
  local copies, waits for them, and re-layouts  12.5 us (4%)
    psum x1, waiting for transfers between devices, broadcast(): return lax.psum(kept, axis)  186 us
    all_to_all x1, blocking collectives, body(): lax.all_to_all(send_buffer.reshape(dev_count, capacity, PB, CB), 'dev', s...  57.6 us
    dot_general x4, matrix products, body(): lax.dot_general(panel_cols, fitted_factors, (((0,), (0,)), ((), ())), pre...  34.7 us
    select_n x1, other arithmetic, broadcast(): jnp.where(lax.axis_index(axis) == source, value, 0).astype(value.dtype)  21.7 us
  transfers between devices with their start and end apart: 1, of which 1 were waited for; matrix products, arithmetic and copies ran while one was open for 0% of the time, Pallas kernels for 0%

commit v1 on v0

v1 whole, which is shorter than its diff:
```python
import functools

import jax
import jax.numpy as jnp
from jax import lax
from jax.experimental import pallas as pl
from jax.experimental.pallas import tpu as pltpu
from jax.sharding import PartitionSpec as P

PB = 256
CB = 128
W = 128
CHUNKS = PB // W
PANELS = 4
C = PANELS * W
NAUX = 9000
HALF = 4608
QUART = HALF // 4
SIXT = QUART // 4
X, Y = 4, 4


def dev_id(x, y, core):
    return ((x % X) * Y + (y % Y)) * 2 + core


def ring_pairs(first, shift):
    pairs = []
    for x in range(X):
        for y in range(Y):
            for core in range(2):
                along_x = first == (core == 0)
                dx, dy = (shift, 0) if along_x else (0, shift)
                pairs.append((dev_id(x, y, core), dev_id(x + dx, y + dy, core)))
    return pairs


CORE_PAIRS = [(d, d ^ 1) for d in range(2 * X * Y)]


def move(value, first, shift):
    return lax.ppermute(value, "dev", ring_pairs(first, shift))


def swap(value):
    return lax.ppermute(value, "dev", CORE_PAIRS)


def pick_kernel(where_ref, *refs):
    ins, (own_ref, send_ref) = refs[:-2], refs[-2:]
    for i in range(PANELS):
        own_ref[:, i * W : (i + 1) * W] = ins[i][...]
        send_ref[:, i * W : (i + 1) * W] = ins[PANELS + i][...]


def pick(factors, col_blocks, core):
    rows = QUART
    steps = HALF // rows
    where = jnp.concatenate([col_blocks, core[None]]).astype(jnp.int32)

    def own_map(i, r, s):
        return (s[PANELS] * steps + r, s[i])

    def other_map(i, r, s):
        return ((1 - s[PANELS]) * steps + r, s[i])

    in_specs = [pl.BlockSpec((rows, W), functools.partial(own_map, i)) for i in range(PANELS)]
    in_specs += [pl.BlockSpec((rows, W), functools.partial(other_map, i)) for i in range(PANELS)]
    out_spec = pl.BlockSpec((rows, C), lambda r, s: (r, 0))
    shape = jax.ShapeDtypeStruct((HALF, C), jnp.bfloat16)
    return pl.pallas_call(
        pick_kernel,
        grid_spec=pltpu.PrefetchScalarGridSpec(
            num_scalar_prefetch=1, grid=(steps,), in_specs=in_specs, out_specs=[out_spec, out_spec]
        ),
        out_shape=[shape, shape],
        compiler_params=pltpu.CompilerParams(vmem_limit_bytes=32 << 20),
        cost_estimate=pl.CostEstimate(flops=0, bytes_accessed=4 * HALF * C * 2, transcendentals=0),
        name="pick_columns",
    )(where, *([factors] * (2 * PANELS)))


def export_kernel(tile_ref, scale_ref, prod_ref, out_ref):
    def slot(s, carry):
        t = tile_ref[s]
        row = pl.multiple_of((t // 8) * W, W)
        col = pl.multiple_of((t % 8) * CB, CB)
        block = prod_ref[pl.ds(row, W), pl.ds(col, CB)]
        out_ref[s] = (block * scale_ref[s]).astype(jnp.bfloat16)
        return carry

    lax.fori_loop(0, out_ref.shape[0], slot, 0)


def to_slots(product, tile_of, scale_of):
    slots = tile_of.shape[0]
    return pl.pallas_call(
        export_kernel,
        in_specs=[
            pl.BlockSpec(memory_space=pltpu.SMEM),
            pl.BlockSpec(memory_space=pltpu.SMEM),
            pl.BlockSpec(memory_space=pltpu.VMEM),
        ],
        out_specs=pl.BlockSpec(memory_space=pltpu.VMEM),
        out_shape=jax.ShapeDtypeStruct((slots, W, CB), jnp.bfloat16),
        compiler_params=pltpu.CompilerParams(vmem_limit_bytes=32 << 20),
        cost_estimate=pl.CostEstimate(
            flops=slots * W * CB, bytes_accessed=product.size * 4 + slots * W * CB * 2, transcendentals=0
        ),
        name="tiles_to_slots",
    )(tile_of, scale_of, product)


def rows_at(value, start, count):
    return lax.dynamic_slice_in_dim(value, start, count, 0)


def scatter_ring(take, size, here, root, first):
    half = size // 2
    far = ((here + 2) % 4) * size
    ahead, behind = (here + 1) % 4, (here + 3) % 4
    from_behind = move(take(far, half), first, 1)
    from_ahead = move(take(far + half, half), first, -1)
    root_behind, root_ahead = root == behind, root == ahead
    forth = jnp.concatenate(
        [jnp.where(root_behind, from_behind, take(ahead * size, half)), take(ahead * size + half, half)], axis=0
    )
    back = jnp.concatenate(
        [take(behind * size, half), jnp.where(root_ahead, from_ahead, take(behind * size + half, half))], axis=0
    )
    got_behind = move(forth, first, 1)
    got_ahead = move(back, first, -1)
    own = take(here * size, size)
    root_here = root == here
    low = jnp.where(root_here, own[:half], jnp.where(root_ahead, got_ahead[:half], got_behind[:half]))
    high = jnp.where(root_here, own[half:], jnp.where(root_behind, got_behind[half:], got_ahead[half:]))
    return jnp.concatenate([low, high], axis=0)


def gather_ring(piece, here, first):
    half = piece.shape[0] // 2
    from_behind = move(piece, first, 1)
    from_ahead = move(piece, first, -1)
    low = move(from_behind[:half], first, 1)
    high = move(from_ahead[half:], first, -1)
    far = jnp.concatenate([low, high], axis=0)
    return [(piece, here), (from_behind, (here + 3) % 4), (from_ahead, (here + 1) % 4), (far, (here + 2) % 4)]


def lay_out(pieces, base, buffer):
    for piece, place in pieces:
        buffer = lax.dynamic_update_slice_in_dim(buffer, piece, base + place * piece.shape[0], 0)
    return buffer


def slot_table(owners, slots, kept):
    count = owners.shape[0]
    same_owner = owners[:, None] == owners[None, :]
    earlier = jnp.arange(count)[None, :] < jnp.arange(count)[:, None]
    ranks = jnp.sum((same_owner & earlier).astype(jnp.int32), axis=-1)
    hit = (owners * 2 + ranks)[None, :] == jnp.arange(slots)[:, None]
    tile_of = jnp.sum(jnp.where(hit, jnp.arange(count)[None, :], 0), axis=1).astype(jnp.int32)
    scale_of = jnp.sum(jnp.where(hit, kept[None, :], 0), axis=1).astype(jnp.float32)
    return tile_of, scale_of


def body(fitted_factors, panel_blocks, kept_tiles, tile_owner):
    me = lax.axis_index("dev")
    core = me % 2
    mx, my = me // (2 * Y), (me // 2) % Y
    here_a, here_b = jnp.where(core == 0, mx, my), jnp.where(core == 0, my, mx)
    root = panel_blocks // 4
    root_x, root_y, root_core = root // (2 * Y), (root // 2) % Y, root % 2

    def per_column(value):
        return jnp.repeat(value, W)[None, :]

    root_a = per_column(jnp.where(core == 0, root_x, root_y))
    root_b = per_column(jnp.where(core == 0, root_y, root_x))
    is_mine = per_column(root_core == core)
    col_blocks = (panel_blocks % 4) * CHUNKS

    slots = 2 * 2 * X * Y
    tile_of, scale_of = slot_table(tile_owner[0, 0, :, 0], slots, kept_tiles.reshape(-1))

    received = []
    for h in range(CHUNKS):
        own, send = pick(fitted_factors, col_blocks + h, core)
        sibling = swap(send)

        def take(start, count):
            return jnp.where(is_mine, rows_at(own, start, count), rows_at(sibling, start, count))

        quart = scatter_ring(take, QUART, here_a, root_a, True)
        sixteenth = scatter_ring(functools.partial(rows_at, quart), SIXT, here_b, root_b, False)
        pieces = gather_ring(sixteenth, here_b, False)
        quart = lay_out(pieces, 0, jnp.zeros((QUART, C), jnp.bfloat16))
        pieces = gather_ring(quart, here_a, True)
        far_a = here_b
        others = [
            (swap(piece), (far_a + off) % 4) for (piece, _), off in zip(pieces, (0, 3, 1, 2), strict=True)
        ]
        panel = lay_out(pieces, core * HALF, jnp.zeros((2 * HALF, C), jnp.bfloat16))
        panel = lay_out(others, (1 - core) * HALF, panel)
        product = lax.dot_general(
            panel[:NAUX], fitted_factors, (((0,), (0,)), ((), ())), preferred_element_type=jnp.float32
        )
        outgoing = to_slots(product, tile_of, scale_of)
        received.append(lax.all_to_all(outgoing, "dev", split_axis=0, concat_axis=0, tiled=True))
    exported = jnp.concatenate(received, axis=1)
    return exported.reshape(1, 1, slots, PB, CB)


def solution(mesh):
    placed = (P(None, "dev"), P("grp"), P("grp", "dev"), P("grp", "dev", None, None))
    return jax.shard_map(
        body,
        mesh=mesh,
        in_specs=placed,
        out_specs=P("grp", "dev", None, None, None),
        check_vma=False,
    )
```

time: 330 us -> 289 us (0.88)
  waiting for transfers between devices: 186 us -> 67.2 us
  starting transfers between devices: 0.01 us -> 72.4 us
  blocking collectives: 57.6 us -> 31.8 us
  local copies, waits for them, and re-layouts: 12.5 us -> 34 us
  Pallas kernels: 0 us -> 20.5 us
  between operations: 16.2 us -> 0.68 us
  other arithmetic: 22.8 us -> 30.5 us
    psum x1 -> x0, waiting for transfers between devices: 186 us -> none  [broadcast(): return lax.psum(kept, axis)]
    ppermute x0 -> x42, starting transfers between devices: none -> 64.1 us  [the longest x32 38.4 us: move(): return lax.ppermute(value, 'dev', ring_pairs(first, shift))]
    ppermute x0 -> x42, waiting for transfers between devices: none -> 58 us  [the longest x32 50.9 us: move(): return lax.ppermute(value, 'dev', ring_pairs(first, shift))]
    all_to_all x1, blocking collectives: 57.6 us -> 31.8 us  [body(): lax.all_to_all(outgoing, 'dev', split_axis=0, concat_axis=0, tiled=True)]
    pallas_call x0 -> x4, Pallas kernels: none -> 20.5 us  [the longest x2 15.1 us: pick(): pl.pallas_call(pick_kernel, grid_spec=pltpu.PrefetchScalarGridSpec(num_sc...]
    dynamic_update_slice x0 -> x20, local copies, waits for them, and re-layouts: none -> 14.8 us  [lay_out(): lax.dynamic_update_slice_in_dim(buffer, piece, base + place * piece.shape...]
    all_to_all x0 -> x1, waiting for transfers between devices: none -> 9.19 us  [body(): lax.all_to_all(outgoing, 'dev', split_axis=0, concat_axis=0, tiled=True)]
    concatenate x1 -> x15, other arithmetic: 0.26 us -> 8.56 us  [the longest x4 3.67 us: scatter_ring(): jnp.concatenate([jnp.where(root_behind, from_behind, take(ahead * size, h...]
  transfers between devices with their start and end apart: 1 -> 43, of which waited for: 1 -> 17; matrix products, arithmetic and copies ran while one was open for 0% -> 25% of each run, Pallas kernels for 0% -> 4%
where the time goes in v1:
time: 289 us
  starting transfers between devices  72.4 us (25%)
  waiting for transfers between devices  67.2 us (23%)
  local copies, waits for them, and re-layouts  34 us (12%)
  matrix products  32 us (11%)
  blocking collectives  31.8 us (11%)
  other arithmetic  30.5 us (11%)
  Pallas kernels  20.5 us (7%)
    ppermute x32, waiting for transfers between devices, move(): return lax.ppermute(value, 'dev', ring_pairs(first, shift))  50.9 us
    ppermute x32, starting transfers between devices, move(): return lax.ppermute(value, 'dev', ring_pairs(first, shift))  38.4 us
    dot_general x2, matrix products, body(): lax.dot_general(panel[:NAUX], fitted_factors, (((0,), (0,)), ((), ())), p...  32 us
    all_to_all x1, blocking collectives, body(): lax.all_to_all(outgoing, 'dev', split_axis=0, concat_axis=0, tiled=True)  31.8 us
    ppermute x10, starting transfers between devices, swap(): return lax.ppermute(value, 'dev', CORE_PAIRS)  25.7 us
    pallas_call x2, Pallas kernels, pick(): pl.pallas_call(pick_kernel, grid_spec=pltpu.PrefetchScalarGridSpec(num_sc...  15.1 us
    dynamic_update_slice x20, local copies, waits for them, and re-layouts, lay_out(): lax.dynamic_update_slice_in_dim(buffer, piece, base + place * piece.shape...  14.8 us
    select_n x3, other arithmetic, take(): jnp.where(is_mine, rows_at(own, start, count), rows_at(sibling, start, co...  11 us
  transfers between devices with their start and end apart: 43, of which 17 were waited for; matrix products, arithmetic and copies ran while one was open for 25% of the time, Pallas kernels for 4%

profile of v1, /device:TPU:1, one launch (start us, length us, event | category | flops | bytes accessed | tf_op | source)
XLA Modules:
  0.0 289.0 jit_solution(8873466669550341609)
XLA Ops:
  0.7 7.6 %pick_columns.2 = (bf16[4608,512]{1,0:T(8,128)(2,1)S(1)}, bf16[4608,512]{1,0:T(8,128)(2,1)}) custom-call(s32[5]{0:T(128)S(1)} %get-tuple-element.74.where_ref, bf16[9000,1024]{1,0:T(8,128)(2,1)} %refs_7_.3, bf16[9000,1024]{1,0:T(8,128)(2,1)} %refs_7_.3, bf16[9000,1024]{1,0:T(8,128)(2,1)} %refs_7_.3, bf16[9000,1024]{1,0:T(8,128)(2,1)} %refs_7_.3, ...), custom_call_target="tpu_custom_call" | custom-call | bytes 18874368 | tf_op jit(solution)/shard_map/pick_columns/pallas_call | solution.py:71
  8.3 2.2 copy-done
  10.5 1.4 collective-permute-start
  11.9 7.6 %pick_columns.3 = (bf16[4608,512]{1,0:T(8,128)(2,1)S(1)}, bf16[4608,512]{1,0:T(8,128)(2,1)}) custom-call(s32[5]{0:T(128)S(1)} %get-tuple-element.75.where_ref, bf16[9000,1024]{1,0:T(8,128)(2,1)} %refs_7_.3, bf16[9000,1024]{1,0:T(8,128)(2,1)} %refs_7_.3, bf16[9000,1024]{1,0:T(8,128)(2,1)} %refs_7_.3, bf16[9000,1024]{1,0:T(8,128)(2,1)} %refs_7_.3, ...), custom_call_target="tpu_custom_call" | custom-call | bytes 18874368 | tf_op jit(solution)/shard_map/pick_columns/pallas_call | solution.py:71
  19.5 2.1 copy-done.2
  22.9 7.0 %collective-permute-done.21 = bf16[4608,512]{1,0:T(8,128)(2,1)} collective-permute-done((bf16[4608,512]{1,0:T(8,128)(2,1)}, bf16[4608,512]{1,0:T(8,128)(2,1)}, u32[]{:S(2)}, u32[]{:S(2)}) %collective-permute-start.21) | collective-permute-done | bytes 4718624 | tf_op jit(solution)/shard_map/ppermute | solution.py:46
  29.9 3.2 %dynamic-slice_select_fusion.8 = (bf16[576,512]{1,0:T(8,128)(2,1)S(1)}, bf16[576,512]{1,0:T(8,128)(2,1)S(1)}, bf16[576,512]{1,0:T(8,128)(2,1)S(1)}, bf16[576,512]{1,0:T(8,128)(2,1)S(1)}) fusion(bf16[4608,512]{1,0:T(8,128)(2,1)} %collective-permute-done, s32[]{:T(128)S(6)} %select_n.397, bf16[4608,512]{1,0:T(8,128)(2,1)} %copy-done, ...), kind=kLoop, calls=%fused_computation.57 | loop fusion | flops 1179648 | bytes 7078408 | tf_op jit(solution)/shard_map/jit(_where)/select_n | solution.py:192
  33.1 2.9 collective-permute-start.1
  37.6 5.2 %collective-permute-done.1 = bf16[576,512]{1,0:T(8,128)(2,1)S(1)} collective-permute-done((bf16[576,512]{1,0:T(8,128)(2,1)S(1)}, bf16[576,512]{1,0:T(8,128)(2,1)S(1)}, u32[]{:S(2)}, u32[]{:S(2)}) %collective-permute-start.1) | collective-permute-done | bytes 589856 | tf_op jit(solution)/shard_map/ppermute | solution.py:42
  42.8 6.3 %collective-permute-done.22 = bf16[576,512]{1,0:T(8,128)(2,1)S(1)} collective-permute-done((bf16[576,512]{1,0:T(8,128)(2,1)S(1)}, bf16[576,512]{1,0:T(8,128)(2,1)S(1)}, u32[]{:S(2)}, u32[]{:S(2)}) %collective-permute-start.22) | collective-permute-done | bytes 589856 | tf_op jit(solution)/shard_map/ppermute | solution.py:42
  49.1 3.9 %collective-permute-done.3 = bf16[576,512]{1,0:T(8,128)(2,1)S(1)} collective-permute-done((bf16[576,512]{1,0:T(8,128)(2,1)S(1)}, bf16[576,512]{1,0:T(8,128)(2,1)S(1)}, u32[]{:S(2)}, u32[]{:S(2)}) %collective-permute-start.3) | collective-permute-done | bytes 589856 | tf_op jit(solution)/shard_map/ppermute | solution.py:42
  53.0 4.8 %dynamic-slice_select_fusion.5 = (bf16[576,512]{1,0:T(8,128)(2,1)S(1)}, bf16[576,512]{1,0:T(8,128)(2,1)S(1)}, bf16[576,512]{1,0:T(8,128)(2,1)S(1)}, bf16[576,512...) fusion(bf16[4608,512]{1,0:T(8,128)(2,1)} %collective-permute-do, ...), kind=kLoop, calls=%fused_computation.52 | loop fusion | flops 3538944 | bytes 16516624 | tf_op jit(solution)/shard_map/jit(_where)/select_n | solution.py:192
  58.8 1.1 pad_maximum_fusion.1
  60.0 1.5 collective-permute-start.4
  61.4 1.1 pad_maximum_fusion.3
  63.6 2.7 collective-permute-start.23
  67.0 3.0 %dynamic-slice_select_fusion.1 = (bf16[1152,512]{1,0:T(8,128)(2,1)S(1)}, bf16[1152,512]{1,0:T(8,128)(2,1)S(1)}) fusion(bf16[4608,512]{1,0:T(8,128)(2,1)} %collective-permute-done, s32[]{:T(128)S(6)} %select_n.390, bf16[4608,512]{1,0:T(8,128)(2,1)} %copy-done, pred[512]{0:T(512)(128)(4,1)S(1)} %broadcast_bitcast_fusion.4, ...), kind=kLoop, calls=%fused_computation.38 | loop fusion | flops 1179648 | bytes 7078404 | tf_op jit(solution)/shard_map/jit(_where)/select_n | solution.py:192
  70.0 4.4 %collective-permute-done.2 = bf16[1152,512]{1,0:T(8,128)(2,1)S(1)} collective-permute-done((bf16[1152,512]{1,0:T(8,128)(2,1)}, bf16[1152,512]{1,0:T(8,128)(2,1)S(1)}, u32[]{:S(2)}, u32[]{:S(2)}) %collective-permute-start.2) | collective-permute-done | bytes 1179680 | tf_op jit(solution)/shard_map/ppermute | solution.py:42
  74.4 2.3 collective-permute-done.4
  76.7 12.6 %collective-permute-done.25 = bf16[1152,512]{1,0:T(8,128)(2,1)S(1)} collective-permute-done((bf16[1152,512]{1,0:T(8,128)(2,1)}, bf16[1152,512]{1,0:T(8,128)(2,1)S(1)}, u32[]{:S(2)}, u32[]{:S(2)}) %collective-permute-start.25) | collective-permute-done | bytes 1179680 | tf_op jit(solution)/shard_map/ppermute | solution.py:42
  90.4 2.5 fusion.4
  94.0 1.3 collective-permute-start.28
  95.3 3.1 %collective-permute-done.7 = bf16[144,512]{1,0:T(8,128)(2,1)S(1)} collective-permute-done((bf16[144,512]{1,0:T(8,128)(2,1)S(1)}, bf16[144,512]{1,0:T(8,128)(2,1)S(1)}, u32[]{:S(2)}, u32[]{:S(2)}) %collective-permute-start.7) | collective-permute-done | bytes 147488 | tf_op jit(solution)/shard_map/ppermute | solution.py:42
  99.3 1.2 collective-permute-start.5
  102.5 1.2 collective-permute-start.8
  106.5 1.8 collective-permute-start.6
  110.0 2.9 %collective-permute-done.29 = bf16[288,512]{1,0:T(8,128)(2,1)S(1)} collective-permute-done((bf16[288,512]{1,0:T(8,128)(2,1)}, bf16[288,512]{1,0:T(8,128)(2,1)S(1)}, u32[]{:S(2)}, u32[]{:S(2)}) %collective-permute-start.29) | collective-permute-done | bytes 294944 | tf_op jit(solution)/shard_map/ppermute | solution.py:42
  113.0 2.8 collective-permute-done.27
  116.6 2.3 collective-permute-start.10
  119.0 2.7 collective-permute-start.31
  121.7 1.2 collective-permute-done.9
  123.0 2.7 collective-permute-start.12
  126.1 3.0 %collective-permute-start.33 = (bf16[144,512]{1,0:T(8,128)(2,1)S(1)}, bf16[144,512]{1,0:T(8,128)(2,1)S(1)}, u32[]{:S(2)}, u32[]{:S(2)}) collective-permute-start(bf16[144,512]{1,0:T(8,128)(2,1)S(1)} %slice.166), channel_id=1, source_target_pairs={{0,6},{1,25},{2,0},{3,27},{4,2},{5,29},{6,4},{7,31},{8,14},{9,1},{... | collective-permute-start | bytes 442376 | tf_op jit(solution)/shard_map/ppermute | solution.py:42
  129.8 2.3 collective-permute-start.14
  132.7 12.7 %collective-permute-start.17 = (bf16[1152,512]{1,0:T(8,128)(2,1)S(1)}, bf16[1152,512]{1,0:T(8,128)(2,1)S(1)}, u32[]{:S(2)}, u32[]{:S(2)}) collective-permute-start(bf16[1152,512]{1,0:T(8,128)(2,1)S(1)} %maximum_dynamic-update-slice_fusion), channel_id=1, source_target_pairs={{0,1},{1,0},{2,3},{3,2},{4,5},{5,4},{6,7},{7,6},{8,9},{9,8},{10,11... | collective-permute-start | bytes 3538952 | tf_op jit(solution)/shard_map/ppermute | solution.py:46
  145.5 3.1 %collective-permute-start.35 = (bf16[1152,512]{1,0:T(8,128)(2,1)S(1)}, bf16[1152,512]{1,0:T(8,128)(2,1)S(1)}, u32[]{:S(2)}, u32[]{:S(2)}) collective-permute-start(bf16[1152,512]{1,0:T(8,128)(2,1)S(1)} %maximum_dynamic-update-slice_fusion.1), channel_id=1, source_target_pairs={{0,24},{1,7},{2,26},{3,1},{4,28},{5,3},{6,30},{7,5},{8,0},{9,15},{... | collective-permute-start | bytes 3538952 | tf_op jit(solution)/shard_map/ppermute | solution.py:42
  148.5 4.1 %broadcast.114.clone.1 = bf16[9216,512]{1,0:T(8,128)(2,1)} broadcast(bf16[]{:T(256)} %constant.182.clone.1), dimensions={} | broadcast | bytes 9437186 | tf_op jit(solution)/shard_map/broadcast.11
  152.7 1.1 constant_dynamic-update-slice_fusion.13
  154.6 1.1 slice.150
  155.9 2.7 collective-permute-start.16
  158.6 3.3 %collective-permute-done.34 = bf16[1152,512]{1,0:T(8,128)(2,1)} collective-permute-done((bf16[1152,512]{1,0:T(8,128)(2,1)S(1)}, bf16[1152,512]{1,0:T(8,128)(2,1)}, u32[]{:S(2)}, u32[]{:S(2)}) %collective-permute-start.34) | collective-permute-done | bytes 1179680 | tf_op jit(solution)/shard_map/ppermute | solution.py:42
  161.9 1.1 slice.167
  163.1 2.4 constant_dynamic-update-slice_fusion.12
  165.5 1.4 constant_dynamic-update-slice_fusion.21
  168.0 7.6 %collective-permute-start.38 = (bf16[1152,512]{1,0:T(8,128)(2,1)S(1)}, bf16[1152,512]{1,0:T(8,128)(2,1)S(1)}, u32[]{:S(2)}, u32[]{:S(2)}) collective-permute-start(bf16[1152,512]{1,0:T(8,128)(2,1)S(1)} %maximum_dynamic-update-slice_fusion.1), channel_id=1, source_target_pairs={{0,1},{1,0},{2,3},{3,2},{4,5},{5,4},{6,7},{7,6},{8,9},{9,8},{10,11... | collective-permute-start | bytes 3538952 | tf_op jit(solution)/shard_map/ppermute | solution.py:46
  175.7 2.6 collective-permute-start.37
  178.3 2.8 collective-permute-start.18
  182.0 1.1 constant_dynamic-update-slice_fusion.10
  183.1 2.0 collective-permute-done.37
  186.5 1.4 constant_dynamic-update-slice_fusion.1
  188.0 1.1 constant_dynamic-update-slice_fusion.9
  189.8 1.1 constant_dynamic-update-slice_fusion.8
  191.1 1.1 constant_dynamic-update-slice_fusion.7
  192.5 3.5 %copy-done.3 = bf16[9216,512]{1,0:T(8,128)(2,1)} copy-done((bf16[9216,512]{1,0:T(8,128)(2,1)}, bf16[9216,512]{1,0:T(8,128)(2,1)S(1)}, u32[]{:S(2)}) %copy-start.3) | copy-done | bytes 9437208
  196.0 1.2 constant_dynamic-update-slice_fusion.6
  197.2 16.0 %fusion.2.prod_ref = f32[512,1024]{1,0:T(8,128)S(1)} fusion(bf16[9000,1024]{1,0:T(8,128)(2,1)} %refs_7_.3, bf16[9216,512]{1,0:T(8,128)(2,1)} %constant_dynamic-update-slice_fusion.6), kind=kOutput, calls=%fused_computation.2 | convolution fusion | flops 9437184000 | bytes 29745152 | tf_op jit(solution)/shard_map/dot_general | solution.py:205
  213.2 3.3 %tiles_to_slots.2 = bf16[64,128,128]{2,1,0:T(8,128)(2,1)} custom-call(s32[64]{0:T(128)S(1)} %get-tuple-element.14.tile_ref, f32[64]{0:T(128)S(1)} %convert_element_type.7.scale_ref, f32[512,1024]{1,0:T(8,128)S(1)} %fusion.2.prod_ref), custom_call_target="tpu_custom_call" | custom-call | flops 1048576 | bytes 4194304 | tf_op jit(solution)/shard_map/tiles_to_slots/pallas_call | solution.py:97
  216.5 8.3 %all-to-all-start = ((bf16[64,128,128]{2,1,0:T(8,128)(2,1)}), bf16[64,128,128]{2,1,0:T(8,128)(2,1)}, u32[]{:S(2)}, u32[]{:S(2)}) async-start(bf16[64,128,128]{2,1,0:T(8,128)(2,1)} %tiles_to_slots.2), calls=%async_computation | async-start | bytes 4194304 | tf_op jit(solution)/shard_map/all_to_all | solution.py:209
  224.8 1.1 constant_dynamic-update-slice_fusion.5
  225.9 16.0 %fusion.prod_ref = f32[512,1024]{1,0:T(8,128)S(1)} fusion(bf16[9000,1024]{1,0:T(8,128)(2,1)} %refs_7_.3, bf16[9216,512]{1,0:T(8,128)(2,1)} %constant_dynamic-update-slice_fusion.5), kind=kOutput, calls=%fused_computation | convolution fusion | flops 9437184000 | bytes 29745152 | tf_op jit(solution)/shard_map/dot_general | solution.py:205
  241.9 2.0 tiles_to_slots.3
  244.0 9.2 %all-to-all-done = bf16[64,128,128]{2,1,0:T(8,128)(2,1)} async-done(((bf16[64,128,128]{2,1,0:T(8,128)(2,1)}), bf16[64,128,128]{2,1,0:T(8,128)(2,1)}, u32[]{:S(2)}, u32[]{:S(2)}) %all-to-all-start) | async-done | bytes 2097184 | tf_op jit(solution)/shard_map/all_to_all | solution.py:209
  253.1 31.8 %all_to_all.10 = bf16[64,128,128]{2,1,0:T(8,128)(2,1)S(1)} all-to-all(bf16[64,128,128]{2,1,0:T(8,128)(2,1)S(1)} %tiles_to_slots.3), channel_id=1, replica_groups=mesh['grp'=4,'dev'=32] {'dev'}, dimensions={0} | all-to-all | bytes 4194304 | tf_op jit(solution)/shard_map/all_to_all | solution.py:209
  284.9 4.1 %maximum_bitcast_fusion = bf16[1,1,64,256,128]{4,3,2,1,0:T(8,128)(2,1)} fusion(bf16[64,128,128]{2,1,0:T(8,128)(2,1)S(1)} %all_to_all.10, bf16[64,128,128]{2,1,0:T(8,128)(2,1)} %all-to-all-done), kind=kLoop, calls=%fused_computation.4 | loop fusion | flops 8388608 | bytes 8388608 | tf_op jit(solution)/shard_map/reshape | solution.py:211
  (130 shorter events, 24.4 us)
Async XLA Ops:
  8.3 2.2 copy-start
  10.5 12.4 %collective-permute-start = (bf16[4608,512]{1,0:T(8,128)(2,1)}, bf16[4608,512]{1,0:T(8,128)(2,1)}, u32[]{:S(2)}, u32[]{:S(2)}) collective-permute-start(bf16[4608,512]{1,0:T(8,128)(2,1)} %get-tuple-element.10), channel_id=1, source_target_pairs={{0,1},{1,0},{2,3},{3,2},{4,5},{5,4},{6,7},{7,6},{8,9},{9,8},{10,11... | collective-permute-start | bytes 14155784 | tf_op jit(solution)/shard_map/ppermute | solution.py:46
  11.9 9.7 %copy-start.7 = (s32[4]{0:T(128)S(1)}, s32[4]{0:T(128)}, u32[]{:S(2)}) copy-start(s32[4]{0:T(128)} %param.5) | copy-start | bytes 52
  19.5 2.1 copy-start.2
  21.6 8.3 %collective-permute-start.21 = (bf16[4608,512]{1,0:T(8,128)(2,1)}, bf16[4608,512]{1,0:T(8,128)(2,1)}, u32[]{:S(2)}, u32[]{:S(2)}) collective-permute-start(bf16[4608,512]{1,0:T(8,128)(2,1)} %get-tuple-element.12), channel_id=1, source_target_pairs={{0,1},{1,0},{2,3},{3,2},{4,5},{5,4},{6,7},{7,6},{8,9},{9,8},{10,11... | collective-permute-start | bytes 14155784 | tf_op jit(solution)/shard_map/ppermute | solution.py:46
  29.9 23.1 %copy-start.1 = (bf16[4608,512]{1,0:T(8,128)(2,1)S(1)}, bf16[4608,512]{1,0:T(8,128)(2,1)}, u32[]{:S(2)}) copy-start(bf16[4608,512]{1,0:T(8,128)(2,1)} %copy-done) | copy-start | bytes 14155780
  33.1 9.7 %collective-permute-start.1 = (bf16[576,512]{1,0:T(8,128)(2,1)S(1)}, bf16[576,512]{1,0:T(8,128)(2,1)S(1)}, u32[]{:S(2)}, u32[]{:S(2)}) collective-permute-start(bf16[576,512]{1,0:T(8,128)(2,1)S(1)} %get-tuple-element.28), channel_id=1, source_target_pairs={{0,24},{1,7},{2,26},{3,1},{4,28},{5,3},{6,30},{7,5},{8,0},{9,15},{... | collective-permute-start | bytes 1769480 | tf_op jit(solution)/shard_map/ppermute | solution.py:42
  36.0 13.1 %collective-permute-start.22 = (bf16[576,512]{1,0:T(8,128)(2,1)S(1)}, bf16[576,512]{1,0:T(8,128)(2,1)S(1)}, u32[]{:S(2)}, u32[]{:S(2)}) collective-permute-start(bf16[576,512]{1,0:T(8,128)(2,1)S(1)} %get-tuple-element.69), channel_id=1, source_target_pairs={{0,24},{1,7},{2,26},{3,1},{4,28},{5,3},{6,30},{7,5},{8,0},{9,15},{... | collective-permute-start | bytes 1769480 | tf_op jit(solution)/shard_map/ppermute | solution.py:42
  36.4 12.7 %collective-permute-start.24 = (bf16[576,512]{1,0:T(8,128)(2,1)S(1)}, bf16[576,512]{1,0:T(8,128)(2,1)S(1)}, u32[]{:S(2)}, u32[]{:S(2)}) collective-permute-start(bf16[576,512]{1,0:T(8,128)(2,1)S(1)} %get-tuple-element.68), channel_id=1, source_target_pairs={{0,8},{1,3},{2,10},{3,5},{4,12},{5,7},{6,14},{7,1},{8,16},{9,11},{... | collective-permute-start | bytes 1769480 | tf_op jit(solution)/shard_map/ppermute | solution.py:42
  37.4 15.6 %collective-permute-start.3 = (bf16[576,512]{1,0:T(8,128)(2,1)S(1)}, bf16[576,512]{1,0:T(8,128)(2,1)S(1)}, u32[]{:S(2)}, u32[]{:S(2)}) collective-permute-start(bf16[576,512]{1,0:T(8,128)(2,1)S(1)} %get-tuple-element.29), channel_id=1, source_target_pairs={{0,8},{1,3},{2,10},{3,5},{4,12},{5,7},{6,14},{7,1},{8,16},{9,11},{... | collective-permute-start | bytes 1769480 | tf_op jit(solution)/shard_map/ppermute | solution.py:42
  58.8 15.6 %collective-permute-start.2 = (bf16[1152,512]{1,0:T(8,128)(2,1)}, bf16[1152,512]{1,0:T(8,128)(2,1)S(1)}, u32[]{:S(2)}, u32[]{:S(2)}) collective-permute-start(bf16[1152,512]{1,0:T(8,128)(2,1)} %pad_maximum_fusion), channel_id=1, source_target_pairs={{0,24},{1,7},{2,26},{3,1},{4,28},{5,3},{6,30},{7,5},{8,0},{9,15},{... | collective-permute-start | bytes 3538952 | tf_op jit(solution)/shard_map/ppermute | solution.py:42
  60.0 16.8 %collective-permute-start.4 = (bf16[1152,512]{1,0:T(8,128)(2,1)}, bf16[1152,512]{1,0:T(8,128)(2,1)S(1)}, u32[]{:S(2)}, u32[]{:S(2)}) collective-permute-start(bf16[1152,512]{1,0:T(8,128)(2,1)} %pad_maximum_fusion.1), channel_id=1, source_target_pairs={{0,8},{1,3},{2,10},{3,5},{4,12},{5,7},{6,14},{7,1},{8,16},{9,11},{... | collective-permute-start | bytes 3538952 | tf_op jit(solution)/shard_map/ppermute | solution.py:42
  62.5 26.8 %collective-permute-start.25 = (bf16[1152,512]{1,0:T(8,128)(2,1)}, bf16[1152,512]{1,0:T(8,128)(2,1)S(1)}, u32[]{:S(2)}, u32[]{:S(2)}) collective-permute-start(bf16[1152,512]{1,0:T(8,128)(2,1)} %pad_maximum_fusion.3), channel_id=1, source_target_pairs={{0,8},{1,3},{2,10},{3,5},{4,12},{5,7},{6,14},{7,1},{8,16},{9,11},{... | collective-permute-start | bytes 3538952 | tf_op jit(solution)/shard_map/ppermute | solution.py:42
  63.6 25.8 %collective-permute-start.23 = (bf16[1152,512]{1,0:T(8,128)(2,1)}, bf16[1152,512]{1,0:T(8,128)(2,1)}, u32[]{:S(2)}, u32[]{:S(2)}) collective-permute-start(bf16[1152,512]{1,0:T(8,128)(2,1)} %pad_maximum_fusion.2), channel_id=1, source_target_pairs={{0,24},{1,7},{2,26},{3,1},{4,28},{5,3},{6,30},{7,5},{8,0},{9,15},{... | collective-permute-start | bytes 3538952 | tf_op jit(solution)/shard_map/ppermute | solution.py:42
  76.7 12.6 %copy-start.4 = (bf16[1152,512]{1,0:T(8,128)(2,1)}, bf16[1152,512]{1,0:T(8,128)(2,1)S(1)}, u32[]{:S(2)}) copy-start(bf16[1152,512]{1,0:T(8,128)(2,1)S(1)} %collective-permute-done.4) | copy-start | bytes 3538948
  89.4 1.0 copy-start.5
  92.9 0.9 copy-start.9
  93.1 5.3 %collective-permute-start.7 = (bf16[144,512]{1,0:T(8,128)(2,1)S(1)}, bf16[144,512]{1,0:T(8,128)(2,1)S(1)}, u32[]{:S(2)}, u32[]{:S(2)}) collective-permute-start(bf16[144,512]{1,0:T(8,128)(2,1)S(1)} %fusion.20), channel_id=1, source_target_pairs={{0,2},{1,9},{2,4},{3,11},{4,6},{5,13},{6,0},{7,15},{8,10},{9,17},{... | collective-permute-start | bytes 442376 | tf_op jit(solution)/shard_map/ppermute | solution.py:42
  94.0 6.6 %collective-permute-start.28 = (bf16[144,512]{1,0:T(8,128)(2,1)S(1)}, bf16[144,512]{1,0:T(8,128)(2,1)S(1)}, u32[]{:S(2)}, u32[]{:S(2)}) collective-permute-start(bf16[144,512]{1,0:T(8,128)(2,1)S(1)} %fusion.14), channel_id=1, source_target_pairs={{0,2},{1,9},{2,4},{3,11},{4,6},{5,13},{6,0},{7,15},{8,10},{9,17},{... | collective-permute-start | bytes 442376 | tf_op jit(solution)/shard_map/ppermute | solution.py:42
  99.3 5.7 %collective-permute-start.5 = (bf16[144,512]{1,0:T(8,128)(2,1)S(1)}, bf16[144,512]{1,0:T(8,128)(2,1)S(1)}, u32[]{:S(2)}, u32[]{:S(2)}) collective-permute-start(bf16[144,512]{1,0:T(8,128)(2,1)S(1)} %get-tuple-element.42), channel_id=1, source_target_pairs={{0,6},{1,25},{2,0},{3,27},{4,2},{5,29},{6,4},{7,31},{8,14},{9,1},{... | collective-permute-start | bytes 442376 | tf_op jit(solution)/shard_map/ppermute | solution.py:42
  101.5 4.1 %collective-permute-start.26 = (bf16[144,512]{1,0:T(8,128)(2,1)S(1)}, bf16[144,512]{1,0:T(8,128)(2,1)S(1)}, u32[]{:S(2)}, u32[]{:S(2)}) collective-permute-start(bf16[144,512]{1,0:T(8,128)(2,1)S(1)} %get-tuple-element.46), channel_id=1, source_target_pairs={{0,6},{1,25},{2,0},{3,27},{4,2},{5,29},{6,4},{7,31},{8,14},{9,1},{... | collective-permute-start | bytes 442376 | tf_op jit(solution)/shard_map/ppermute | solution.py:42
  102.5 7.5 %collective-permute-start.8 = (bf16[288,512]{1,0:T(8,128)(2,1)}, bf16[288,512]{1,0:T(8,128)(2,1)S(1)}, u32[]{:S(2)}, u32[]{:S(2)}) collective-permute-start(bf16[288,512]{1,0:T(8,128)(2,1)} %pad_maximum_fusion.5), channel_id=1, source_target_pairs={{0,2},{1,9},{2,4},{3,11},{4,6},{5,13},{6,0},{7,15},{8,10},{9,17},{... | collective-permute-start | bytes 884744 | tf_op jit(solution)/shard_map/ppermute | solution.py:42
  104.5 8.5 %collective-permute-start.29 = (bf16[288,512]{1,0:T(8,128)(2,1)}, bf16[288,512]{1,0:T(8,128)(2,1)S(1)}, u32[]{:S(2)}, u32[]{:S(2)}) collective-permute-start(bf16[288,512]{1,0:T(8,128)(2,1)} %pad_maximum_fusion.8), channel_id=1, source_target_pairs={{0,2},{1,9},{2,4},{3,11},{4,6},{5,13},{6,0},{7,15},{8,10},{9,17},{... | collective-permute-start | bytes 884744 | tf_op jit(solution)/shard_map/ppermute | solution.py:42
  105.8 3.4 %copy-start.8 = (pred[4]{0:T(512)(128)(4,1)S(1)}, pred[4]{0:T(512)(128)(4,1)}, u32[]{:S(2)}) copy-start(pred[4]{0:T(512)(128)(4,1)} %get-tuple-element.15) | copy-start | bytes 16
  106.5 6.4 %collective-permute-start.6 = (bf16[288,512]{1,0:T(8,128)(2,1)}, bf16[288,512]{1,0:T(8,128)(2,1)S(1)}, u32[]{:S(2)}, u32[]{:S(2)}) collective-permute-start(bf16[288,512]{1,0:T(8,128)(2,1)} %pad_maximum_fusion.4), channel_id=1, source_target_pairs={{0,6},{1,25},{2,0},{3,27},{4,2},{5,29},{6,4},{7,31},{8,14},{9,1},{... | collective-permute-start | bytes 884744 | tf_op jit(solution)/shard_map/ppermute | solution.py:42
  109.0 6.7 %collective-permute-start.27 = (bf16[288,512]{1,0:T(8,128)(2,1)}, bf16[288,512]{1,0:T(8,128)(2,1)S(1)}, u32[]{:S(2)}, u32[]{:S(2)}) collective-permute-start(bf16[288,512]{1,0:T(8,128)(2,1)} %pad_maximum_fusion.7), channel_id=1, source_target_pairs={{0,6},{1,25},{2,0},{3,27},{4,2},{5,29},{6,4},{7,31},{8,14},{9,1},{... | collective-permute-start | bytes 884744 | tf_op jit(solution)/shard_map/ppermute | solution.py:42
  116.0 6.9 %collective-permute-start.9 = (bf16[288,512]{1,0:T(8,128)(2,1)S(1)}, bf16[288,512]{1,0:T(8,128)(2,1)S(1)}, u32[]{:S(2)}, u32[]{:S(2)}) collective-permute-start(bf16[288,512]{1,0:T(8,128)(2,1)S(1)} %get-tuple-element.52), channel_id=1, source_target_pairs={{0,2},{1,9},{2,4},{3,11},{4,6},{5,13},{6,0},{7,15},{8,10},{9,17},{... | collective-permute-start | bytes 884744 | tf_op jit(solution)/shard_map/ppermute | solution.py:42
  116.6 6.4 %collective-permute-start.10 = (bf16[288,512]{1,0:T(8,128)(2,1)S(1)}, bf16[288,512]{1,0:T(8,128)(2,1)S(1)}, u32[]{:S(2)}, u32[]{:S(2)}) collective-permute-start(bf16[288,512]{1,0:T(8,128)(2,1)S(1)} %get-tuple-element.52), channel_id=1, source_target_pairs={{0,6},{1,25},{2,0},{3,27},{4,2},{5,29},{6,4},{7,31},{8,14},{9,1},{... | collective-permute-start | bytes 884744 | tf_op jit(solution)/shard_map/ppermute | solution.py:42
  119.0 7.1 %collective-permute-start.30 = (bf16[288,512]{1,0:T(8,128)(2,1)S(1)}, bf16[288,512]{1,0:T(8,128)(2,1)S(1)}, u32[]{:S(2)}, u32[]{:S(2)}) collective-permute-start(bf16[288,512]{1,0:T(8,128)(2,1)S(1)} %get-tuple-element.54), channel_id=1, source_target_pairs={{0,2},{1,9},{2,4},{3,11},{4,6},{5,13},{6,0},{7,15},{8,10},{9,17},{... | collective-permute-start | bytes 884744 | tf_op jit(solution)/shard_map/ppermute | solution.py:42
  119.0 7.1 %collective-permute-start.31 = (bf16[288,512]{1,0:T(8,128)(2,1)S(1)}, bf16[288,512]{1,0:T(8,128)(2,1)S(1)}, u32[]{:S(2)}, u32[]{:S(2)}) collective-permute-start(bf16[288,512]{1,0:T(8,128)(2,1)S(1)} %get-tuple-element.54), channel_id=1, source_target_pairs={{0,6},{1,25},{2,0},{3,27},{4,2},{5,29},{6,4},{7,31},{8,14},{9,1},{... | collective-permute-start | bytes 884744 | tf_op jit(solution)/shard_map/ppermute | solution.py:42
  122.9 6.4 %collective-permute-start.11 = (bf16[144,512]{1,0:T(8,128)(2,1)S(1)}, bf16[144,512]{1,0:T(8,128)(2,1)S(1)}, u32[]{:S(2)}, u32[]{:S(2)}) collective-permute-start(bf16[144,512]{1,0:T(8,128)(2,1)S(1)} %slice.148), channel_id=1, source_target_pairs={{0,2},{1,9},{2,4},{3,11},{4,6},{5,13},{6,0},{7,15},{8,10},{9,17},{... | collective-permute-start | bytes 442376 | tf_op jit(solution)/shard_map/ppermute | solution.py:42
  123.0 6.3 %collective-permute-start.12 = (bf16[144,512]{1,0:T(8,128)(2,1)S(1)}, bf16[144,512]{1,0:T(8,128)(2,1)S(1)}, u32[]{:S(2)}, u32[]{:S(2)}) collective-permute-start(bf16[144,512]{1,0:T(8,128)(2,1)S(1)} %slice.149), channel_id=1, source_target_pairs={{0,6},{1,25},{2,0},{3,27},{4,2},{5,29},{6,4},{7,31},{8,14},{9,1},{... | collective-permute-start | bytes 442376 | tf_op jit(solution)/shard_map/ppermute | solution.py:42
  126.0 6.1 %collective-permute-start.32 = (bf16[144,512]{1,0:T(8,128)(2,1)S(1)}, bf16[144,512]{1,0:T(8,128)(2,1)S(1)}, u32[]{:S(2)}, u32[]{:S(2)}) collective-permute-start(bf16[144,512]{1,0:T(8,128)(2,1)S(1)} %slice.165), channel_id=1, source_target_pairs={{0,2},{1,9},{2,4},{3,11},{4,6},{5,13},{6,0},{7,15},{8,10},{9,17},{... | collective-permute-start | bytes 442376 | tf_op jit(solution)/shard_map/ppermute | solution.py:42
  126.1 6.0 %collective-permute-start.33 = (bf16[144,512]{1,0:T(8,128)(2,1)S(1)}, bf16[144,512]{1,0:T(8,128)(2,1)S(1)}, u32[]{:S(2)}, u32[]{:S(2)}) collective-permute-start(bf16[144,512]{1,0:T(8,128)(2,1)S(1)} %slice.166), channel_id=1, source_target_pairs={{0,6},{1,25},{2,0},{3,27},{4,2},{5,29},{6,4},{7,31},{8,14},{9,1},{... | collective-permute-start | bytes 442376 | tf_op jit(solution)/shard_map/ppermute | solution.py:42
  129.2 3.1 %copy-start.6 = (s32[4,8]{1,0:T(4,128)S(1)}, s32[4,8]{1,0:T(4,128)}, u32[]{:S(2)}) copy-start(s32[4,8]{1,0:T(4,128)} %param.6) | copy-start | bytes 388
  129.2 3.2 %copy-start.10 = (s32[1,1,32,1]{2,3,1,0:T(1,128)S(1)}, s32[1,1,32,1]{2,3,1,0:T(1,128)}, u32[]{:S(2)}) copy-start(s32[1,1,32,1]{2,3,1,0:T(1,128)} %param.7) | copy-start | bytes 388
  129.4 25.2 %collective-permute-start.13 = (bf16[1152,512]{1,0:T(8,128)(2,1)S(1)}, bf16[1152,512]{1,0:T(8,128)(2,1)}, u32[]{:S(2)}, u32[]{:S(2)}) collective-permute-start(bf16[1152,512]{1,0:T(8,128)(2,1)S(1)} %maximum_dynamic-update-slice_fusion), channel_id=1, source_target_pairs={{0,8},{1,3},{2,10},{3,5},{4,12},{5,7},{6,14},{7,1},{8,16},{9,11},{... | collective-permute-start | bytes 3538952 | tf_op jit(solution)/shard_map/ppermute | solution.py:42
  129.8 26.0 %collective-permute-start.14 = (bf16[1152,512]{1,0:T(8,128)(2,1)S(1)}, bf16[1152,512]{1,0:T(8,128)(2,1)S(1)}, u32[]{:S(2)}, u32[]{:S(2)}) collective-permute-start(bf16[1152,512]{1,0:T(8,128)(2,1)S(1)} %maximum_dynamic-update-slice_fusion), channel_id=1, source_target_pairs={{0,24},{1,7},{2,26},{3,1},{4,28},{5,3},{6,30},{7,5},{8,0},{9,15},{... | collective-permute-start | bytes 3538952 | tf_op jit(solution)/shard_map/ppermute | solution.py:42
  132.1 29.8 %collective-permute-start.34 = (bf16[1152,512]{1,0:T(8,128)(2,1)S(1)}, bf16[1152,512]{1,0:T(8,128)(2,1)}, u32[]{:S(2)}, u32[]{:S(2)}) collective-permute-start(bf16[1152,512]{1,0:T(8,128)(2,1)S(1)} %maximum_dynamic-update-slice_fusion.1), channel_id=1, source_target_pairs={{0,8},{1,3},{2,10},{3,5},{4,12},{5,7},{6,14},{7,1},{8,16},{9,11},{... | collective-permute-start | bytes 3538952 | tf_op jit(solution)/shard_map/ppermute | solution.py:42
  132.7 55.1 %collective-permute-start.17 = (bf16[1152,512]{1,0:T(8,128)(2,1)S(1)}, bf16[1152,512]{1,0:T(8,128)(2,1)S(1)}, u32[]{:S(2)}, u32[]{:S(2)}) collective-permute-start(bf16[1152,512]{1,0:T(8,128)(2,1)S(1)} %maximum_dynamic-update-slice_fusion), channel_id=1, source_target_pairs={{0,1},{1,0},{2,3},{3,2},{4,5},{5,4},{6,7},{7,6},{8,9},{9,8},{10,11... | collective-permute-start | bytes 3538952 | tf_op jit(solution)/shard_map/ppermute | solution.py:46
  145.5 22.5 %collective-permute-start.35 = (bf16[1152,512]{1,0:T(8,128)(2,1)S(1)}, bf16[1152,512]{1,0:T(8,128)(2,1)S(1)}, u32[]{:S(2)}, u32[]{:S(2)}) collective-permute-start(bf16[1152,512]{1,0:T(8,128)(2,1)S(1)} %maximum_dynamic-update-slice_fusion.1), channel_id=1, source_target_pairs={{0,24},{1,7},{2,26},{3,1},{4,28},{5,3},{6,30},{7,5},{8,0},{9,15},{... | collective-permute-start | bytes 3538952 | tf_op jit(solution)/shard_map/ppermute | solution.py:42
  155.7 20.0 %collective-permute-start.15 = (bf16[576,512]{1,0:T(8,128)(2,1)S(1)}, bf16[576,512]{1,0:T(8,128)(2,1)S(1)}, u32[]{:S(2)}, u32[]{:S(2)}) collective-permute-start(bf16[576,512]{1,0:T(8,128)(2,1)S(1)} %slice.150), channel_id=1, source_target_pairs={{0,8},{1,3},{2,10},{3,5},{4,12},{5,7},{6,14},{7,1},{8,16},{9,11},{... | collective-permute-start | bytes 1769480 | tf_op jit(solution)/shard_map/ppermute | solution.py:42
  155.9 26.1 %collective-permute-start.16 = (bf16[576,512]{1,0:T(8,128)(2,1)S(1)}, bf16[576,512]{1,0:T(8,128)(2,1)S(1)}, u32[]{:S(2)}, u32[]{:S(2)}) collective-permute-start(bf16[576,512]{1,0:T(8,128)(2,1)S(1)} %slice.151), channel_id=1, source_target_pairs={{0,24},{1,7},{2,26},{3,1},{4,28},{5,3},{6,30},{7,5},{8,0},{9,15},{... | collective-permute-start | bytes 1769480 | tf_op jit(solution)/shard_map/ppermute | solution.py:42
  163.0 15.3 %collective-permute-start.36 = (bf16[576,512]{1,0:T(8,128)(2,1)S(1)}, bf16[576,512]{1,0:T(8,128)(2,1)S(1)}, u32[]{:S(2)}, u32[]{:S(2)}) collective-permute-start(bf16[576,512]{1,0:T(8,128)(2,1)S(1)} %slice.167), channel_id=1, source_target_pairs={{0,8},{1,3},{2,10},{3,5},{4,12},{5,7},{6,14},{7,1},{8,16},{9,11},{... | collective-permute-start | bytes 1769480 | tf_op jit(solution)/shard_map/ppermute | solution.py:42
  168.0 21.1 %collective-permute-start.38 = (bf16[1152,512]{1,0:T(8,128)(2,1)S(1)}, bf16[1152,512]{1,0:T(8,128)(2,1)S(1)}, u32[]{:S(2)}, u32[]{:S(2)}) collective-permute-start(bf16[1152,512]{1,0:T(8,128)(2,1)S(1)} %maximum_dynamic-update-slice_fusion.1), channel_id=1, source_target_pairs={{0,1},{1,0},{2,3},{3,2},{4,5},{5,4},{6,7},{7,6},{8,9},{9,8},{10,11... | collective-permute-start | bytes 3538952 | tf_op jit(solution)/shard_map/ppermute | solution.py:46
  175.7 9.4 %collective-permute-start.37 = (bf16[576,512]{1,0:T(8,128)(2,1)S(1)}, bf16[576,512]{1,0:T(8,128)(2,1)S(1)}, u32[]{:S(2)}, u32[]{:S(2)}) collective-permute-start(bf16[576,512]{1,0:T(8,128)(2,1)S(1)} %slice.168), channel_id=1, source_target_pairs={{0,24},{1,7},{2,26},{3,1},{4,28},{5,3},{6,30},{7,5},{8,0},{9,15},{... | collective-permute-start | bytes 1769480 | tf_op jit(solution)/shard_map/ppermute | solution.py:42
  178.3 11.4 %collective-permute-start.18 = (bf16[1152,512]{1,0:T(8,128)(2,1)}, bf16[1152,512]{1,0:T(8,128)(2,1)S(1)}, u32[]{:S(2)}, u32[]{:S(2)}) collective-permute-start(bf16[1152,512]{1,0:T(8,128)(2,1)} %collective-permute-done.13), channel_id=1, source_target_pairs={{0,1},{1,0},{2,3},{3,2},{4,5},{5,4},{6,7},{7,6},{8,9},{9,8},{10,11... | collective-permute-start | bytes 3538952 | tf_op jit(solution)/shard_map/ppermute | solution.py:46
  181.9 9.2 %collective-permute-start.19 = (bf16[1152,512]{1,0:T(8,128)(2,1)S(1)}, bf16[1152,512]{1,0:T(8,128)(2,1)S(1)}, u32[]{:S(2)}, u32[]{:S(2)}) collective-permute-start(bf16[1152,512]{1,0:T(8,128)(2,1)S(1)} %collective-permute-done.14), channel_id=1, source_target_pairs={{0,1},{1,0},{2,3},{3,2},{4,5},{5,4},{6,7},{7,6},{8,9},{9,8},{10,11... | collective-permute-start | bytes 3538952 | tf_op jit(solution)/shard_map/ppermute | solution.py:46
  185.1 5.9 %collective-permute-start.39 = (bf16[1152,512]{1,0:T(8,128)(2,1)}, bf16[1152,512]{1,0:T(8,128)(2,1)S(1)}, u32[]{:S(2)}, u32[]{:S(2)}) collective-permute-start(bf16[1152,512]{1,0:T(8,128)(2,1)} %collective-permute-done.34), channel_id=1, source_target_pairs={{0,1},{1,0},{2,3},{3,2},{4,5},{5,4},{6,7},{7,6},{8,9},{9,8},{10,11... | collective-permute-start | bytes 3538952 | tf_op jit(solution)/shard_map/ppermute | solution.py:46
  187.9 4.3 %collective-permute-start.40 = (bf16[1152,512]{1,0:T(8,128)(2,1)S(1)}, bf16[1152,512]{1,0:T(8,128)(2,1)S(1)}, u32[]{:S(2)}, u32[]{:S(2)}) collective-permute-start(bf16[1152,512]{1,0:T(8,128)(2,1)S(1)} %collective-permute-done.35), channel_id=1, source_target_pairs={{0,1},{1,0},{2,3},{3,2},{4,5},{5,4},{6,7},{7,6},{8,9},{9,8},{10,11... | collective-permute-start | bytes 3538952 | tf_op jit(solution)/shard_map/ppermute | solution.py:46
  189.1 3.4 %collective-permute-start.20 = (bf16[1152,512]{1,0:T(8,128)(2,1)S(1)}, bf16[1152,512]{1,0:T(8,128)(2,1)S(1)}, u32[]{:S(2)}, u32[]{:S(2)}) collective-permute-start(bf16[1152,512]{1,0:T(8,128)(2,1)S(1)} %constant_dynamic-update-slice_fusion.22), channel_id=1, source_target_pairs={{0,1},{1,0},{2,3},{3,2},{4,5},{5,4},{6,7},{7,6},{8,9},{9,8},{10,11... | collective-permute-start | bytes 3538952 | tf_op jit(solution)/shard_map/ppermute | solution.py:46
  189.7 35.0 %collective-permute-start.41 = (bf16[1152,512]{1,0:T(8,128)(2,1)}, bf16[1152,512]{1,0:T(8,128)(2,1)S(1)}, u32[]{:S(2)}, u32[]{:S(2)}) collective-permute-start(bf16[1152,512]{1,0:T(8,128)(2,1)} %constant_dynamic-update-slice_fusion.24), channel_id=1, source_target_pairs={{0,1},{1,0},{2,3},{3,2},{4,5},{5,4},{6,7},{7,6},{8,9},{9,8},{10,11... | collective-permute-start | bytes 3538952 | tf_op jit(solution)/shard_map/ppermute | solution.py:46
  192.3 3.7 %copy-start.3 = (bf16[9216,512]{1,0:T(8,128)(2,1)}, bf16[9216,512]{1,0:T(8,128)(2,1)S(1)}, u32[]{:S(2)}) copy-start(bf16[9216,512]{1,0:T(8,128)(2,1)S(1)} %constant_dynamic-update-slice_fusion.4) | copy-start | bytes 28311556
  216.5 36.6 %all-to-all-start = ((bf16[64,128,128]{2,1,0:T(8,128)(2,1)}), bf16[64,128,128]{2,1,0:T(8,128)(2,1)}, u32[]{:S(2)}, u32[]{:S(2)}) async-start(bf16[64,128,128]{2,1,0:T(8,128)(2,1)} %tiles_to_slots.2), calls=%async_computation | async-start | bytes 4194304 | tf_op jit(solution)/shard_map/all_to_all | solution.py:209
